TPU v7x, 256 devices: a whole 4x4x8 slice. The times are simulated.
256 devices in a mesh: stn: 64 (over z, y_hi, x), chan: 4 (over y_lo, core).
Axes of the slice: x: 4, y: 4 (y_hi: 2, y_lo: 2; y = y_hi * 2 + y_lo), z: 8, core: 2. Of those that a mesh axis runs over, the one named last changes fastest.
Arguments:
- samples: bfloat16 [512, 17, 2, 8192], P(('stn', 'chan')), may hold values from -6 to 6
- keeper: int32 [64, 64], replicated, may hold values from 0 to 1, as said below
Outputs:
- visibilities: bfloat16 [512, 2, 4096, 264], P('stn', None, 'chan')
Inputs may be any that keep to these rules, and one draw needn't show every extreme that they name: keeper[g, g] is 1; for g != h with d = (g - h) mod 64: keeper[g, h] is 1 where 0 < d < 32, 0 where d > 32, and at d = 32 exactly one of keeper[g, h] and keeper[h, g] is 1, which one drawn for each such pair; half of the rows hold 33 ones, the others 33 - 1.
All inputs are finite; a program needn't handle non-finite values.
Results may differ from a plain program's by a relative error of at most 0.0077.
Values may be sent and summed in bfloat16 or wider, within the bound.
No kernel may reach another device: no remote copies, remote signals or barrier semaphores. Data moves between devices by JAX's collectives and lax.ppermute only.
A program may use at most 192 MiB of HBM per device.

v0:
```python
import math
import jax
import jax.numpy as jnp
from jax import lax
from jax.sharding import PartitionSpec as P

NFFT = 8192
TAPS = 16
CH_WIN = 1024
DFT_BLOCK = 256


def taps_table():
    pos = jnp.arange(TAPS * NFFT).astype(jnp.float32)
    shifted = (pos + 0.5) / NFFT - TAPS / 2.0
    window = 0.5 - 0.5 * jnp.cos(2.0 * math.pi * (pos + 0.5) / (TAPS * NFFT))
    return (jnp.sinc(shifted) * window).reshape(TAPS, NFFT)


def twiddles(width):
    index_n = jnp.arange(NFFT, dtype=jnp.int32)[:, None]
    index_k = jnp.arange(width, dtype=jnp.int32)[None, :]
    phase = (index_n * index_k % NFFT).astype(jnp.float32) * (2.0 * math.pi / NFFT)
    cosines = jnp.cos(phase).astype(jnp.bfloat16)
    sines = jnp.sin(phase).astype(jnp.bfloat16)
    upper = jnp.concatenate([cosines, -sines], axis=1)
    lower = jnp.concatenate([sines, cosines], axis=1)
    return jnp.concatenate([upper, lower], axis=0)


def rotations(ch_tot, width):
    blocks = ch_tot // width
    index_n = jnp.arange(NFFT, dtype=jnp.int32)[None, :]
    index_b = jnp.arange(blocks, dtype=jnp.int32)[:, None]
    phase = (index_n * index_b * width % NFFT).astype(jnp.float32) * (2.0 * math.pi / NFFT)
    return (jnp.cos(phase), jnp.sin(phase))


def channelise(block, taps, table, cos_rot, sin_rot, ch_tot):
    frames = block.shape[1] - TAPS + 1
    count = block.shape[0]
    width = table.shape[1] // 2
    blocks = ch_tot // width
    total = taps[0] * block[:, 0:frames].astype(jnp.float32)
    for tap in range(1, TAPS):
        total = total + taps[tap] * block[:, tap : tap + frames].astype(jnp.float32)
    real_part = total[:, :, 0][None]
    imag_part = total[:, :, 1][None]
    cosine = cos_rot[:, None, None, :]
    sine = sin_rot[:, None, None, :]
    rot_real = real_part * cosine + imag_part * sine
    rot_imag = imag_part * cosine - real_part * sine
    lhs = jnp.stack([rot_real, rot_imag], axis=3).astype(jnp.bfloat16)
    lhs = lhs.reshape(blocks * count * frames, 2 * NFFT)
    spectrum = jnp.dot(lhs, table, preferred_element_type=jnp.float32) * (1.0 / math.sqrt(NFFT))
    spectrum = spectrum.astype(jnp.bfloat16).reshape(blocks, count, frames, 2, width)
    spectrum = jnp.transpose(spectrum, (1, 0, 4, 3, 2))
    return spectrum.reshape(count, ch_tot, 2, frames)


def correlate(own, others, frames):
    half = others.shape[2] // 2
    turned = jnp.concatenate([-others[:, :, half:], others[:, :, :half]], axis=2)
    rhs = jnp.concatenate([others, turned], axis=0)
    product = lax.dot_general(
        own, rhs, (((2,), (2,)), ((1,), (1,))), preferred_element_type=jnp.float32
    )
    rows = others.shape[0]
    product = product.reshape(product.shape[0], product.shape[1], 2, rows)
    return jnp.transpose(product, (1, 2, 0, 3)) / frames


def slot_table(keep_rows, keep_slots):
    ranking = jnp.cumsum(keep_rows, axis=1) - 1
    slot_index = jnp.arange(keep_slots, dtype=jnp.int32)
    matched = (keep_rows[:, :, None] == 1) & (ranking[:, :, None] == slot_index[None, None, :])
    column_ids = jnp.arange(keep_rows.shape[1], dtype=jnp.int32)
    slot_column = jnp.sum(jnp.where(matched, column_ids[None, :, None], 0), axis=1)
    filled = jnp.any(matched, axis=1)
    return (slot_column, filled)


def per_device(samples, keeper):
    n_chan = lax.axis_size("chan")
    n_stn = lax.axis_size("stn")
    ch_tot = CH_WIN * n_chan
    frames = samples.shape[1] - TAPS + 1
    cos_rot, sin_rot = rotations(ch_tot, DFT_BLOCK)
    spectrum = channelise(samples, taps_table(), twiddles(DFT_BLOCK), cos_rot, sin_rot, ch_tot)
    local = lax.all_to_all(spectrum, "chan", split_axis=1, concat_axis=0, tiled=True)
    group_in = local.shape[0]
    own = local.reshape(group_in, CH_WIN, 2 * frames)
    keep_slots = n_stn // 2 + 1
    group_index = lax.axis_index("stn")
    row_keep = jnp.take(keeper, group_index, axis=0)
    slot_column, filled = slot_table(row_keep[None], keep_slots)
    slot_column = slot_column[0]
    filled = filled[0]
    nothing = jnp.zeros((), jnp.bfloat16)
    col_mask = jnp.repeat(row_keep, group_in).astype(jnp.float32)
    tile = correlate(own, lax.all_gather(own, "stn", axis=0, tiled=True), frames)
    whole = (tile * col_mask[None, None, None, :]).astype(jnp.bfloat16)
    whole = whole.reshape(group_in, 2, CH_WIN, n_stn, group_in)
    picked = jnp.take(whole, slot_column, axis=3)
    picked = jnp.where(filled[None, None, None, :, None], picked, nothing)
    return picked.reshape(group_in, 2, CH_WIN, keep_slots * group_in)


def solution(mesh):
    placed = (P(("stn", "chan"), None, None, None), P())
    return jax.shard_map(
        per_device,
        mesh=mesh,
        in_specs=placed,
        out_specs=P("stn", None, "chan", None),
        check_vma=False,
    )
```

profile of v0, /device:TPU:2, one launch (start us, length us, event | category | flops | bytes accessed | tf_op | source)
XLA Modules:
  0.0 386.7 jit_solution(5526646558050877336)
XLA Ops:
  6.5 2.4 fusion.33
  8.9 2.1 fusion.45
  11.0 35.0 %sine_convert_fusion = (bf16[8192,256]{1,0:T(8,128)(2,1)}, bf16[8192,256]{1,0:T(8,128)(2,1)}) fusion(), kind=kLoop, calls=%fused_computation.25 | loop fusion | flops 33554432 | bytes 8388608 | tf_op jit(solution)/shard_map/convert_element_type | solution.py:25
  46.0 32.4 %fusion.22 = bf16[8192,256]{1,0:T(8,128)(2,1)} fusion(), kind=kLoop, calls=%fused_computation.34 | loop fusion | flops 37748736 | bytes 4194304 | tf_op jit(solution)/shard_map/neg | solution.py:26
  78.4 2.1 multiply_add_fusion.1
  81.0 4.4 %add_convert_fusion = (bf16[16,2,2,1,8192]{4,3,2,1,0:T(2,128)(2,1)S(1)}, bf16[16,2,2,1,8192]{4,3,2,1,0:T(2,128)(2,1)S(1)}) fusion(f32[16,8192]{1,0:T(8,128)S(1)} %get-tuple-element.42, f32[2,2,8192]{2,1,0:T(2,128)S(1)} %get-tuple-element.40, f32[16,8192]{1,0:T(8,128)S(1)} %get-tuple-element.43, f32[2,2,8192]{2,1,0:T(2,128)S(1)} %get-tuple-element.41), kind=kLoop, calls=%fused_computation.33 | loop fusion | flops 4194304 | bytes 3407872 | tf_op jit(solution)/shard_map/convert
  85.4 4.8 %pad_maximum_fusion = bf16[16,2,2,2,8192]{4,3,2,1,0:T(2,128)(2,1)S(1)} fusion(bf16[16,2,2,1,8192]{4,3,2,1,0:T(2,128)(2,1)S(1)} %get-tuple-element.21, bf16[16,2,2,1,8192]{4,3,2,1,0:T(2,128)(2,1)S(1)} %get-tuple-element.20), kind=kLoop, calls=%fused_computation.31 | loop fusion | flops 4194304 | bytes 4194304 | tf_op jit(solution)/shard_map/stack | solution.py:53
  90.2 1.2 copy.51
  91.4 13.7 %fusion.26 = bf16[64,512]{1,0:T(8,128)(2,1)S(1)} fusion(bf16[64,16384]{1,0:T(8,128)(2,1)S(1)} %bitcast.44, bf16[8192,256]{1,0:T(8,128)(2,1)} %get-tuple-element.45, bf16[8192,256]{1,0:T(8,128)(2,1)} %get-tuple-element.44, bf16[8192,256]{1,0:T(8,128)(2,1)} %fusion.22), kind=kOutput, calls=%fused_computation.36 | convolution fusion | flops 1140916224 | bytes 14745600 | tf_op jit(solution)/shard_map/dot_general | solution.py:55
  105.2 4.8 %copy.46 = bf16[2,16,256,2,2]{4,3,0,2,1:T(2,128)(2,1)} copy(bf16[2,16,256,2,2]{2,1,4,3,0:T(8,128)(2,1)S(1)} %bitcast.45) | data formatting | bytes 131072 | tf_op jit(solution)/shard_map/reshape | solution.py:58
  110.0 7.2 %reshape.361 = bf16[4,2,4096]{2,1,0:T(2,128)(2,1)S(1)} reshape(bf16[4096,2,2,2]{3,2,1,0:T(2,128)(2,1)} %bitcast.41) | data formatting | bytes 131072
  117.2 6.8 %all_to_all.15 = bf16[4,2,4096]{2,1,0:T(2,128)(2,1)S(1)} all-to-all(bf16[4,2,4096]{2,1,0:T(2,128)(2,1)S(1)} %reshape.361), channel_id=1, replica_groups=mesh['stn'=64,'chan'=4] {'chan'}, dimensions={0} | all-to-all | bytes 131072 | tf_op jit(solution)/shard_map/all_to_all | solution.py:90
  123.9 10.0 %reshape.362 = bf16[4096,2,2,2]{3,2,1,0:T(2,128)(2,1)} reshape(bf16[4,2,4096]{2,1,0:T(2,128)(2,1)S(1)} %all_to_all.15) | data formatting | bytes 131072
  133.9 9.7 %copy.47 = bf16[2,4,1024,2,2]{2,1,4,3,0:T(4,128)(2,1)S(1)} copy(bf16[2,4,1024,2,2]{4,3,0,2,1:T(2,128)(2,1)} %bitcast.42) | data formatting | bytes 131072 | tf_op jit(solution)/shard_map/all_to_all | solution.py:90
  145.7 0.7 select_reduce_fusion
  149.3 125.9 %all-gather.2.cloned.1.call-done = bf16[512,1024,4]{1,2,0:T(4,128)(2,1)} async-done(((bf16[8,1024,4]{1,2,0:T(4,128)(2,1)}), bf16[512,1024,4]{1,2,0:T(4,128)(2,1)}) %all-gather.2.cloned.1.call-update) | async-done | bytes 4194320 | tf_op jit(solution)/shard_map/all_gather | solution.py:101
  275.2 10.1 %copy.41 = bf16[512,1024,4]{0,2,1:T(4,128)(2,1)} copy(bf16[512,1024,4]{1,2,0:T(4,128)(2,1)} %all-gather.2.cloned.1.call-done) | data formatting | bytes 8388608 | tf_op jit(solution)/shard_map/all_gather | solution.py:101
  285.3 7.7 %slice_negate_fusion = (bf16[512,1024,2]{0,2,1:T(2,128)(2,1)S(1)}, bf16[512,1024,2]{0,2,1:T(2,128)(2,1)S(1)}) fusion(bf16[512,1024,4]{0,2,1:T(4,128)(2,1)} %copy.41), kind=kLoop, calls=%fused_computation.30 | loop fusion | flops 1048576 | bytes 8388608 | tf_op jit(solution)/shard_map/neg | solution.py:63
  293.1 13.0 %fusion.13 = f32[1024,8,1024]{2,1,0:T(8,128)} fusion(bf16[8,1024,4]{0,2,1:T(4,128)(2,1)S(1)} %copy.42, bf16[512,1024,2]{0,2,1:T(2,128)(2,1)S(1)} %get-tuple-element.19, bf16[512,1024,2]{0,2,1:T(2,128)(2,1)S(1)} %get-tuple-element.18, bf16[512,1024,4]{0,2,1:T(4,128)(2,1)S(1)} %copy-done), kind=kOutput, calls=%fused_computation.19 | convolution fusion | flops 92274688 | bytes 42008576 | tf_op jit(solution)/shard_map/dot_general | solution.py:65
  306.1 32.2 %copy.43 = f32[1024,8,2,512]{0,3,2,1:T(8,128)} copy(f32[1024,8,2,512]{3,1,2,0:T(8,128)} %bitcast.40) | data formatting | bytes 67108864 | tf_op jit(solution)/shard_map/reshape | solution.py:69
  338.3 13.4 %fusion = bf16[8,2,1024,64,8]{2,4,3,1,0:T(8,128)(2,1)S(1)} fusion(f32[1024,8,2,512]{0,3,2,1:T(8,128)} %copy.43, f32[512]{0:T(512)S(1)} %mul.838), kind=kLoop, calls=%fused_computation.2 | loop fusion | flops 16777216 | bytes 50333696 | tf_op jit(solution)/shard_map/reshape | solution.py:103
  351.7 7.0 %copy.44 = bf16[8,2,1024,64,8]{2,4,1,0,3:T(8,128)(2,1)} copy(bf16[8,2,1024,64,8]{2,4,3,1,0:T(8,128)(2,1)S(1)} %fusion) | data formatting | bytes 33554432 | tf_op jit(solution)/shard_map/reshape | solution.py:103
  358.7 10.9 %gather_fusion = bf16[33,8,2,1024,8]{3,4,2,1,0:T(8,128)(2,1)} fusion(bf16[8,2,1024,64,8]{2,4,1,0,3:T(8,128)(2,1)} %copy.44, s32[1024]{0:T(1024)S(1)} %pad_clamp_fusion), kind=kCustom, calls=%fused_computation | custom fusion | bytes 17301636 | tf_op jit(solution)/shard_map/jit(_take)/gather | solution.py:104
  369.6 10.3 %fusion.9 = bf16[8,2,1024,264]{2,3,1,0:T(8,128)(2,1)} fusion(pred[264]{0:T(512)(128)(4,1)S(1)} %copy-done.2, pred[264]{0:T(512)(128)(4,1)S(1)} %copy-done.3, bf16[33,8,2,1024,8]{3,4,2,1,0:T(8,128)(2,1)} %gather_fusion), kind=kLoop, calls=%fused_computation.15 | loop fusion | flops 8650752 | bytes 17302032 | tf_op jit(solution)/shard_map/jit(_where)/select_n | solution.py:105
  (34 shorter events, 5.4 us)
Async XLA Ops:
  6.5 71.9 %copy-start.1 = (bf16[2,17,2,8192]{3,2,1,0:T(2,128)(2,1)S(1)}, bf16[2,17,2,8192]{3,2,1,0:T(2,128)(2,1)}, u32[]{:S(2)}) copy-start(bf16[2,17,2,8192]{3,2,1,0:T(2,128)(2,1)} %param.2) | copy-start | bytes 3342340
  6.5 268.7 %all-gather.2.cloned.1.call-start = ((), (), s32[]{:S(2)}) async-start(), calls=%async_computation.1 | async-start | bytes 4259840 | tf_op jit(solution)/shard_map/all_gather | solution.py:101
  285.3 7.8 %copy-start = (bf16[512,1024,4]{0,2,1:T(4,128)(2,1)S(1)}, bf16[512,1024,4]{0,2,1:T(4,128)(2,1)}, u32[]{:S(2)}) copy-start(bf16[512,1024,4]{0,2,1:T(4,128)(2,1)} %copy.41) | copy-start | bytes 12582916
  358.7 10.9 %copy-start.2 = (pred[264]{0:T(512)(128)(4,1)S(1)}, pred[264]{0:T(512)(128)(4,1)}, u32[]{:S(2)}) copy-start(pred[264]{0:T(512)(128)(4,1)} %broadcast_in_dim.82) | copy-start | bytes 796
  358.7 10.9 %copy-start.3 = (pred[264]{0:T(512)(128)(4,1)S(1)}, pred[264]{0:T(512)(128)(4,1)}, u32[]{:S(2)}) copy-start(pred[264]{0:T(512)(128)(4,1)} %broadcast_in_dim.77) | copy-start | bytes 796
Sparse Core Ops, SparseCore 0:
  144.6 130.5 all-gather.1
where the time goes:
time: 388 us; the launch traced here: 387 us
  waiting for transfers between devices  126 us (32%)
  other arithmetic  117 us (30%)
  local copies, waits for them, and re-layouts  96.8 us (25%)
  matrix products  26.7 us (7%)
  between operations  13.6 us (4%)
  blocking collectives  6.77 us (2%)
    all_gather x1, waiting for transfers between devices, per_device(): lax.all_gather(own, 'stn', axis=0, tiled=True)  126 us
    convert_element_type x1, other arithmetic, twiddles(): sines = jnp.sin(phase).astype(jnp.bfloat16)  35 us
    neg x1, other arithmetic, twiddles(): upper = jnp.concatenate([cosines, -sines], axis=1)  32.4 us
    reshape x1, local copies, waits for them, and re-layouts, correlate(): product = product.reshape(product.shape[0], product.shape[1], 2, rows)  32.2 us
    unnamed x12, local copies, waits for them, and re-layouts  18.6 us
    dot_general x1, matrix products, channelise(): jnp.dot(lhs, table, preferred_element_type=jnp.float32)  13.7 us
    reshape x1, other arithmetic, per_device(): whole = whole.reshape(group_in, 2, CH_WIN, n_stn, group_in)  13.4 us
    dot_general x1, matrix products, correlate(): lax.dot_general(own, rhs, (((2,), (2,)), ((1,), (1,))), preferred_element...  13 us
  transfers between devices with their start and end apart: 1, of which 1 were waited for; matrix products, arithmetic and copies ran while one was open for 1% of the time, Pallas kernels for 0%

commit v1 on v0

--- a/solution.py
+++ b/solution.py
@@ -98,7 +98,19 @@
     filled = filled[0]
     nothing = jnp.zeros((), jnp.bfloat16)
     col_mask = jnp.repeat(row_keep, group_in).astype(jnp.float32)
-    tile = correlate(own, lax.all_gather(own, "stn", axis=0, tiled=True), frames)
+
+    def track_the_arrays(work_x, dimension_no):
+        return jnp.concatenate(
+            lax.all_to_all(
+                jnp.stack([work_x] * lax.axis_size("stn"), 0),
+                split_axis=0,
+                axis_name="stn",
+                concat_axis=0,
+            ),
+            dimension_no,
+        )
+
+    tile = correlate(own, track_the_arrays(own, 0), frames)
     whole = (tile * col_mask[None, None, None, :]).astype(jnp.bfloat16)
     whole = whole.reshape(group_in, 2, CH_WIN, n_stn, group_in)
     picked = jnp.take(whole, slot_column, axis=3)

time: 388 us -> 358 us (0.923)
  waiting for transfers between devices: 126 us -> 89.6 us
  starting transfers between devices: 0.01 us -> 14.6 us
  between operations: 13.6 us -> 0.19 us
  local copies, waits for them, and re-layouts: 96.8 us -> 101 us
    all_gather x1 -> x0, waiting for transfers between devices: 126 us -> none  [per_device(): lax.all_gather(own, 'stn', axis=0, tiled=True)]
    all_to_all x0 -> x1, waiting for transfers between devices: none -> 89.6 us  [track_the_arrays(): lax.all_to_all(jnp.stack([work_x] * lax.axis_size('stn'), 0), split_axis=...]
    all_to_all x0 -> x1, starting transfers between devices: none -> 14.6 us  [track_the_arrays(): lax.all_to_all(jnp.stack([work_x] * lax.axis_size('stn'), 0), split_axis=...]
    all_gather x1 -> x0, local copies, waits for them, and re-layouts: 10.1 us -> none  [per_device(): lax.all_gather(own, 'stn', axis=0, tiled=True)]
    reshape x0 -> x1, local copies, waits for them, and re-layouts: none -> 7.84 us  [track_the_arrays(): jnp.concatenate(lax.all_to_all(jnp.stack([work_x] * lax.axis_size('stn'),...]
    all_to_all x0 -> x1, local copies, waits for them, and re-layouts: none -> 4.79 us  [track_the_arrays(): lax.all_to_all(jnp.stack([work_x] * lax.axis_size('stn'), 0), split_axis=...]
where the time goes in v1:
time: 358 us; the launch traced here: 356 us
  other arithmetic  117 us (33%)
  local copies, waits for them, and re-layouts  101 us (28%)
  waiting for transfers between devices  89.6 us (25%)
  matrix products  26.7 us (7%)
  starting transfers between devices  14.6 us (4%)
  blocking collectives  6.77 us (2%)
    all_to_all x1, waiting for transfers between devices, track_the_arrays(): lax.all_to_all(jnp.stack([work_x] * lax.axis_size('stn'), 0), split_axis=...  89.6 us
    convert_element_type x1, other arithmetic, twiddles(): sines = jnp.sin(phase).astype(jnp.bfloat16)  35 us
    neg x1, other arithmetic, twiddles(): upper = jnp.concatenate([cosines, -sines], axis=1)  32.4 us
    reshape x1, local copies, waits for them, and re-layouts, correlate(): product = product.reshape(product.shape[0], product.shape[1], 2, rows)  32.2 us
    unnamed x12, local copies, waits for them, and re-layouts  18.6 us
    all_to_all x1, starting transfers between devices, track_the_arrays(): lax.all_to_all(jnp.stack([work_x] * lax.axis_size('stn'), 0), split_axis=...  14.6 us
    dot_general x1, matrix products, channelise(): jnp.dot(lhs, table, preferred_element_type=jnp.float32)  13.7 us
    reshape x1, other arithmetic, per_device(): whole = whole.reshape(group_in, 2, CH_WIN, n_stn, group_in)  13.4 us
  transfers between devices with their start and end apart: 1, of which 1 were waited for; matrix products, arithmetic and copies ran while one was open for 1% of the time, Pallas kernels for 0%

profile of v1, /device:TPU:2, one launch (start us, length us, event | category | flops | bytes accessed | tf_op | source)
XLA Modules:
  0.0 355.7 jit_solution(2182086236013867504)
XLA Ops:
  0.0 2.4 fusion.33
  4.5 35.0 %sine_convert_fusion = (bf16[8192,256]{1,0:T(8,128)(2,1)}, bf16[8192,256]{1,0:T(8,128)(2,1)}) fusion(), kind=kLoop, calls=%fused_computation.25 | loop fusion | flops 33554432 | bytes 8388608 | tf_op jit(solution)/shard_map/convert_element_type | solution.py:25
  39.5 32.4 %fusion.22 = bf16[8192,256]{1,0:T(8,128)(2,1)} fusion(), kind=kLoop, calls=%fused_computation.35 | loop fusion | flops 37748736 | bytes 4194304 | tf_op jit(solution)/shard_map/neg | solution.py:26
  71.9 2.1 multiply_add_fusion.1
  74.4 4.4 %add_convert_fusion = (bf16[16,2,2,1,8192]{4,3,2,1,0:T(2,128)(2,1)S(1)}, bf16[16,2,2,1,8192]{4,3,2,1,0:T(2,128)(2,1)S(1)}) fusion(f32[16,8192]{1,0:T(8,128)S(1)} %get-tuple-element.42, f32[2,2,8192]{2,1,0:T(2,128)S(1)} %get-tuple-element.40, f32[16,8192]{1,0:T(8,128)S(1)} %get-tuple-element.43, f32[2,2,8192]{2,1,0:T(2,128)S(1)} %get-tuple-element.41), kind=kLoop, calls=%fused_computation.34 | loop fusion | flops 4194304 | bytes 3407872 | tf_op jit(solution)/shard_map/convert
  78.8 4.8 %pad_maximum_fusion = bf16[16,2,2,2,8192]{4,3,2,1,0:T(2,128)(2,1)S(1)} fusion(bf16[16,2,2,1,8192]{4,3,2,1,0:T(2,128)(2,1)S(1)} %get-tuple-element.21, bf16[16,2,2,1,8192]{4,3,2,1,0:T(2,128)(2,1)S(1)} %get-tuple-element.20), kind=kLoop, calls=%fused_computation.32 | loop fusion | flops 4194304 | bytes 4194304 | tf_op jit(solution)/shard_map/stack | solution.py:53
  84.9 13.7 %fusion.26 = bf16[64,512]{1,0:T(8,128)(2,1)S(1)} fusion(bf16[64,16384]{1,0:T(8,128)(2,1)S(1)} %bitcast.48, bf16[8192,256]{1,0:T(8,128)(2,1)} %get-tuple-element.45, bf16[8192,256]{1,0:T(8,128)(2,1)} %get-tuple-element.44, bf16[8192,256]{1,0:T(8,128)(2,1)} %fusion.22), kind=kOutput, calls=%fused_computation.37 | convolution fusion | flops 1140916224 | bytes 14745600 | tf_op jit(solution)/shard_map/dot_general | solution.py:55
  98.6 4.8 %copy.50 = bf16[2,16,256,2,2]{4,3,0,2,1:T(2,128)(2,1)} copy(bf16[2,16,256,2,2]{2,1,4,3,0:T(8,128)(2,1)S(1)} %bitcast.49) | data formatting | bytes 131072 | tf_op jit(solution)/shard_map/reshape | solution.py:58
  103.4 7.2 %reshape.368 = bf16[4,2,4096]{2,1,0:T(2,128)(2,1)S(1)} reshape(bf16[4096,2,2,2]{3,2,1,0:T(2,128)(2,1)} %bitcast.44) | data formatting | bytes 131072
  110.6 6.8 %all_to_all.20 = bf16[4,2,4096]{2,1,0:T(2,128)(2,1)S(1)} all-to-all(bf16[4,2,4096]{2,1,0:T(2,128)(2,1)S(1)} %reshape.368), channel_id=1, replica_groups=mesh['stn'=64,'chan'=4] {'chan'}, dimensions={0} | all-to-all | bytes 131072 | tf_op jit(solution)/shard_map/all_to_all | solution.py:90
  117.4 10.0 %reshape.369 = bf16[4096,2,2,2]{3,2,1,0:T(2,128)(2,1)} reshape(bf16[4,2,4096]{2,1,0:T(2,128)(2,1)S(1)} %all_to_all.20) | data formatting | bytes 131072
  127.4 9.7 %copy.51 = bf16[2,4,1024,2,2]{2,1,4,3,0:T(4,128)(2,1)S(1)} copy(bf16[2,4,1024,2,2]{4,3,0,2,1:T(2,128)(2,1)} %bitcast.45) | data formatting | bytes 131072 | tf_op jit(solution)/shard_map/all_to_all | solution.py:90
  137.2 2.5 stack.10
  139.8 14.6 %all-to-all-start.1 = ((bf16[64,8,1024,4]{2,1,3,0:T(8,128)(2,1)}), bf16[64,8,1024,4]{2,1,3,0:T(8,128)(2,1)}, u32[]{:S(2)}, u32[]{:S(2)}) async-start(bf16[64,8,1024,4]{2,1,3,0:T(8,128)(2,1)} %stack.10), calls=%async_computation.1 | async-start | bytes 8388608 | tf_op jit(solution)/shard_map/all_to_all | solution.py:104
  159.1 89.6 %all-to-all-done.1 = bf16[64,8,1024,4]{2,1,3,0:T(8,128)(2,1)} async-done(((bf16[64,8,1024,4]{2,1,3,0:T(8,128)(2,1)}), bf16[64,8,1024,4]{2,1,3,0:T(8,128)(2,1)}, u32[]{:S(2)}, u32[]{:S(2)}) %all-to-all-start.1) | async-done | bytes 4194336 | tf_op jit(solution)/shard_map/all_to_all | solution.py:104
  248.7 4.8 %copy.61 = bf16[64,8,1024,4]{2,1,0,3:T(8,128)(2,1)} copy(bf16[64,8,1024,4]{2,1,3,0:T(8,128)(2,1)} %all-to-all-done.1) | data formatting | bytes 8388608 | tf_op jit(solution)/shard_map/all_to_all | solution.py:104
  253.5 7.8 %copy.45 = bf16[512,1024,4]{0,2,1:T(4,128)(2,1)} copy(bf16[512,1024,4]{1,0,2:T(8,128)(2,1)} %bitcast.46) | data formatting | bytes 8388608 | tf_op jit(solution)/shard_map/reshape | solution.py:103
  261.3 7.6 %slice_negate_fusion = (bf16[512,1024,2]{0,2,1:T(2,128)(2,1)S(1)}, bf16[512,1024,2]{0,2,1:T(2,128)(2,1)S(1)}) fusion(bf16[512,1024,4]{0,2,1:T(4,128)(2,1)} %copy.45), kind=kLoop, calls=%fused_computation.31 | loop fusion | flops 1048576 | bytes 8388608 | tf_op jit(solution)/shard_map/neg | solution.py:63
  268.9 13.0 %fusion.13 = f32[1024,8,1024]{2,1,0:T(8,128)} fusion(bf16[8,1024,4]{0,2,1:T(4,128)(2,1)S(1)} %copy.46, bf16[512,1024,2]{0,2,1:T(2,128)(2,1)S(1)} %get-tuple-element.19, bf16[512,1024,2]{0,2,1:T(2,128)(2,1)S(1)} %get-tuple-element.18, bf16[512,1024,4]{0,2,1:T(4,128)(2,1)S(1)} %copy-done), kind=kOutput, calls=%fused_computation.19 | convolution fusion | flops 92274688 | bytes 42008576 | tf_op jit(solution)/shard_map/dot_general | solution.py:65
  281.9 32.2 %copy.47 = f32[1024,8,2,512]{0,3,2,1:T(8,128)} copy(f32[1024,8,2,512]{3,1,2,0:T(8,128)} %bitcast.43) | data formatting | bytes 67108864 | tf_op jit(solution)/shard_map/reshape | solution.py:69
  314.1 13.4 %fusion = bf16[8,2,1024,64,8]{2,4,3,1,0:T(8,128)(2,1)S(1)} fusion(f32[1024,8,2,512]{0,3,2,1:T(8,128)} %copy.47, f32[512]{0:T(512)S(1)} %mul.838), kind=kLoop, calls=%fused_computation.2 | loop fusion | flops 16777216 | bytes 50333696 | tf_op jit(solution)/shard_map/reshape | solution.py:115
  327.5 7.0 %copy.48 = bf16[8,2,1024,64,8]{2,4,1,0,3:T(8,128)(2,1)} copy(bf16[8,2,1024,64,8]{2,4,3,1,0:T(8,128)(2,1)S(1)} %fusion) | data formatting | bytes 33554432 | tf_op jit(solution)/shard_map/reshape | solution.py:115
  334.5 10.9 %gather_fusion = bf16[33,8,2,1024,8]{3,4,2,1,0:T(8,128)(2,1)} fusion(bf16[8,2,1024,64,8]{2,4,1,0,3:T(8,128)(2,1)} %copy.48, s32[1024]{0:T(1024)S(1)} %pad_clamp_fusion), kind=kCustom, calls=%fused_computation | custom fusion | bytes 17301636 | tf_op jit(solution)/shard_map/jit(_take)/gather | solution.py:116
  345.4 10.3 %fusion.9 = bf16[8,2,1024,264]{2,3,1,0:T(8,128)(2,1)} fusion(pred[264]{0:T(512)(128)(4,1)S(1)} %copy-done.2, pred[264]{0:T(512)(128)(4,1)S(1)} %copy-done.3, bf16[33,8,2,1024,8]{3,4,2,1,0:T(8,128)(2,1)} %gather_fusion), kind=kLoop, calls=%fused_computation.15 | loop fusion | flops 8650752 | bytes 17302032 | tf_op jit(solution)/shard_map/jit(_where)/select_n | solution.py:117
  (34 shorter events, 8.5 us)
Async XLA Ops:
  0.0 71.9 %copy-start.1 = (bf16[2,17,2,8192]{3,2,1,0:T(2,128)(2,1)S(1)}, bf16[2,17,2,8192]{3,2,1,0:T(2,128)(2,1)}, u32[]{:S(2)}) copy-start(bf16[2,17,2,8192]{3,2,1,0:T(2,128)(2,1)} %param.2) | copy-start | bytes 3342340
  139.8 108.9 %all-to-all-start.1 = ((bf16[64,8,1024,4]{2,1,3,0:T(8,128)(2,1)}), bf16[64,8,1024,4]{2,1,3,0:T(8,128)(2,1)}, u32[]{:S(2)}, u32[]{:S(2)}) async-start(bf16[64,8,1024,4]{2,1,3,0:T(8,128)(2,1)} %stack.10), calls=%async_computation.1 | async-start | bytes 8388608 | tf_op jit(solution)/shard_map/all_to_all | solution.py:104
  261.3 7.6 %copy-start = (bf16[512,1024,4]{0,2,1:T(4,128)(2,1)S(1)}, bf16[512,1024,4]{0,2,1:T(4,128)(2,1)}, u32[]{:S(2)}) copy-start(bf16[512,1024,4]{0,2,1:T(4,128)(2,1)} %copy.45) | copy-start | bytes 12582916
  334.5 10.9 %copy-start.2 = (pred[264]{0:T(512)(128)(4,1)S(1)}, pred[264]{0:T(512)(128)(4,1)}, u32[]{:S(2)}) copy-start(pred[264]{0:T(512)(128)(4,1)} %broadcast_in_dim.82) | copy-start | bytes 796
  334.5 10.9 %copy-start.3 = (pred[264]{0:T(512)(128)(4,1)S(1)}, pred[264]{0:T(512)(128)(4,1)}, u32[]{:S(2)}) copy-start(pred[264]{0:T(512)(128)(4,1)} %broadcast_in_dim.77) | copy-start | bytes 796
